TPU v7x, 512 devices: a whole 4x8x8 slice. The times are simulated.
512 devices in a mesh: ctx: 32 (over y_hi, z, core), tp: 16 (over y_lo, x).
Axes of the slice: x: 4, y: 8 (y_hi: 2, y_lo: 4; y = y_hi * 4 + y_lo), z: 8, core: 2. Of those that a mesh axis runs over, the one named last changes fastest.
Arguments:
- queries: bfloat16 [4096, 8192], P('ctx', 'tp'), may hold values from -6 to 6
- keys_in: bfloat16 [4096, 8192], P('ctx', 'tp'), may hold values from -6 to 6
- values_in: bfloat16 [4096, 8192], P('ctx', 'tp'), may hold values from -6 to 6
- decay_rates: float32 [8192, 16], P('tp'), may hold values from 7.324219e-05 to 0.03
- residues: float32 [8192, 16], P('tp'), may hold values from -1.5 to 1.5
- skip_gain: float32 [8192], P('tp'), may hold values from -4 to 4
- cotangent: bfloat16 [4096, 8192], P('ctx', 'tp'), may hold values from -6 to 6
Outputs:
- operator_out: bfloat16 [4096, 8192], P('ctx', 'tp')
- grad_queries: bfloat16 [4096, 8192], P('ctx', 'tp')
- grad_keys: bfloat16 [4096, 8192], P('ctx', 'tp')
- grad_values: bfloat16 [4096, 8192], P('ctx', 'tp')
- grad_residues: float32 [8192, 16], P('tp')
All inputs are finite; a program needn't handle non-finite values.
Results may differ from a plain program's by a relative error of at most 0.0054.
Values may be sent and summed in bfloat16 or wider, within the bound.
A program may use at most 64 MiB of HBM per device.

v0:
```python
from functools import partial
import math
import jax
import jax.numpy as jnp
from jax import lax
from jax.sharding import PartitionSpec as P

D = 8192
ORDER = 16
PRECISE = lax.Precision.HIGHEST


def chain_link(earlier_pair, later_pair):
    return (earlier_pair[0] * later_pair[0], later_pair[0] * earlier_pair[1] + later_pair[1])


def prepare(decay, weight, block_len):
    positions = jnp.arange(block_len + 1, dtype=jnp.float32)
    powers = jnp.exp(-decay[None] * positions[:, None, None])
    unit_scale = jnp.sqrt(1.0 - jnp.exp(-2.0 * decay))
    mode_coef = weight * unit_scale
    short_filter = jnp.einsum("kcn,cn->kc", powers[:block_len], mode_coef, precision=PRECISE)
    lag_table = jnp.arange(block_len)[:, None] - jnp.arange(block_len)[None, :]
    toeplitz = jnp.where((lag_table >= 0)[:, :, None], short_filter[jnp.maximum(lag_table, 0)], 0.0)
    return (positions, powers, unit_scale, mode_coef, toeplitz, lag_table)


def forward_states(in_blocks, powers, decay, carry_in, block_len):
    block_count = in_blocks.shape[0]
    end_states = jnp.einsum("bsc,scn->bcn", in_blocks, powers[:block_len][::-1], precision=PRECISE)
    decays = jnp.broadcast_to(powers[block_len], end_states.shape)
    _, totals = lax.associative_scan(chain_link, (decays, end_states), axis=0)
    distance = block_len * jnp.arange(1, block_count + 1, dtype=jnp.float32)
    states = totals + jnp.exp(-decay[None] * distance[:, None, None]) * carry_in[None]
    before = jnp.concatenate([carry_in[None], states[:-1]], 0)
    return (before, totals[-1])


def backward_states(back_blocks, powers, decay, carry_back, block_len):
    block_count = back_blocks.shape[0]
    start_states = jnp.einsum("btc,tcn->bcn", back_blocks, powers[:block_len], precision=PRECISE)
    decays = jnp.broadcast_to(powers[block_len], start_states.shape)
    _, totals = lax.associative_scan(chain_link, (decays[::-1], start_states[::-1]), axis=0)
    totals = totals[::-1]
    distance = block_len * jnp.arange(block_count, 0, -1, dtype=jnp.float32)
    states = totals + jnp.exp(-decay[None] * distance[:, None, None]) * carry_back[None]
    after = jnp.concatenate([states[1:], carry_back[None]], 0)
    return (after, totals[0])


def forward_work(lines, tables, block_len):
    decay, weight, carry_in = tables
    positions, powers, unit_scale, mode_coef, toeplitz, lag_table = prepare(
        decay, weight, block_len
    )
    in_blocks = lines[0].reshape(-1, block_len, lines[0].shape[1])
    before, _ = forward_states(in_blocks, powers, decay, carry_in, block_len)
    within_block = jnp.einsum("bsc,tsc->btc", in_blocks, toeplitz, precision=PRECISE)
    from_carry = jnp.einsum("bcn,tcn->btc", before, powers[1:] * mode_coef[None], precision=PRECISE)
    return (within_block + from_carry).reshape(lines[0].shape)


def backward_work(lines, tables, block_len):
    decay, weight, carry_in, carry_back = tables
    positions, powers, unit_scale, mode_coef, toeplitz, lag_table = prepare(
        decay, weight, block_len
    )
    in_blocks = lines[0].reshape(-1, block_len, lines[0].shape[1])
    back_blocks = lines[1].reshape(-1, block_len, lines[1].shape[1])
    before, _ = forward_states(in_blocks, powers, decay, carry_in, block_len)
    after, _ = backward_states(back_blocks, powers, decay, carry_back, block_len)
    within_block = jnp.einsum("btc,tsc->bsc", back_blocks, toeplitz, precision=PRECISE)
    from_carry = jnp.einsum(
        "bcn,scn->bsc", after, powers[1:][::-1] * mode_coef[None], precision=PRECISE
    )
    adjoint = (within_block + from_carry).reshape(lines[1].shape)
    carried = jnp.einsum("btc,tcn,bcn->cn", back_blocks, powers[1:], before, precision=PRECISE)
    pairs = jnp.einsum("btc,bsc->tsc", back_blocks, in_blocks, precision=PRECISE)
    pairs = jnp.where((lag_table >= 0)[:, :, None], pairs, 0.0)
    rising = jnp.exp(decay[None] * positions[:block_len, None, None])
    inside = jnp.einsum("tsc,tcn,scn->cn", pairs, powers[:block_len], rising, precision=PRECISE)
    return (adjoint, unit_scale * (carried + inside))


def to_groups(line_array, group_width):
    seq_rows, channels = line_array.shape
    return jnp.moveaxis(line_array.reshape(seq_rows, channels // group_width, group_width), 1, 0)


def from_groups(stacked):
    group_count, seq_rows, group_width = stacked.shape
    return jnp.moveaxis(stacked, 0, 1).reshape(seq_rows, group_count * group_width)


def param_groups(param_table, group_width):
    return param_table.reshape(
        param_table.shape[0] // group_width, group_width, param_table.shape[1]
    )


def grouped(work_fn, lines, tables, group_width):
    stacked_lines = tuple((to_groups(item, group_width) for item in lines))
    stacked_tables = tuple((param_groups(item, group_width) for item in tables))
    return lax.map(lambda packed: work_fn(packed[0], packed[1]), (stacked_lines, stacked_tables))


def flat_table(stacked):
    return stacked.reshape(stacked.shape[0] * stacked.shape[1], stacked.shape[2])


def shards(queries, keys_in, values_in, decay_rates, residues, skip_gain, cotangent):
    seq_rows, channels = queries.shape
    mode_count = decay_rates.shape[1]
    queries_f = queries.astype(jnp.float32)
    keys_f = keys_in.astype(jnp.float32)
    values_f = values_in.astype(jnp.float32)
    cot_f = cotangent.astype(jnp.float32)
    gated = lax.optimization_barrier((keys_f * values_f).astype(jnp.bfloat16))
    pulled = lax.optimization_barrier((cot_f * queries_f).astype(jnp.bfloat16))
    ctx_count = lax.axis_size("ctx")
    piece_width = channels // ctx_count
    offset = lax.axis_index("ctx") * piece_width
    own_rates = lax.dynamic_slice_in_dim(decay_rates, offset, piece_width, 0)
    own_residues = lax.dynamic_slice_in_dim(residues, offset, piece_width, 0)
    block_len = math.gcd(seq_rows * ctx_count, 128)
    group_width = math.gcd(piece_width, 64)
    zero_state = jnp.zeros((piece_width, mode_count), jnp.float32)
    line_in = lax.all_to_all(gated, "ctx", split_axis=1, concat_axis=0, tiled=True).astype(
        jnp.float32
    )
    conv_line = from_groups(
        grouped(
            partial(forward_work, block_len=block_len),
            (line_in,),
            (own_rates, own_residues, zero_state),
            group_width,
        )
    )
    convolved = lax.all_to_all(
        conv_line.astype(jnp.bfloat16), "ctx", split_axis=0, concat_axis=1, tiled=True
    )
    line_back = lax.all_to_all(pulled, "ctx", split_axis=1, concat_axis=0, tiled=True).astype(
        jnp.float32
    )
    adj_line, raw_grad = grouped(
        partial(backward_work, block_len=block_len),
        (line_in, line_back),
        (own_rates, own_residues, zero_state, zero_state),
        group_width,
    )
    adjoint = lax.all_to_all(
        from_groups(adj_line).astype(jnp.bfloat16), "ctx", split_axis=0, concat_axis=1, tiled=True
    )
    own_raw = flat_table(raw_grad)
    mixed = convolved.astype(jnp.float32) + skip_gain[None, :] * gated.astype(jnp.float32)
    operator_out = (queries_f * mixed).astype(jnp.bfloat16)
    grad_queries = (cot_f * mixed).astype(jnp.bfloat16)
    grad_gated = adjoint.astype(jnp.float32) + skip_gain[None, :] * pulled.astype(jnp.float32)
    grad_keys = (grad_gated * values_f).astype(jnp.bfloat16)
    grad_values = (grad_gated * keys_f).astype(jnp.bfloat16)
    raw_all = lax.all_gather(own_raw, "ctx", axis=0, tiled=True)
    grad_square = lax.psum(jnp.sum(raw_all * raw_all), "tp")
    factor = jnp.minimum(1.0, math.sqrt(D * ORDER) / jnp.sqrt(grad_square + 1e-06))
    grad_residues = raw_all * factor
    return (operator_out, grad_queries, grad_keys, grad_values, grad_residues)


def solution(mesh):
    in_specs = (
        P("ctx", "tp"),
        P("ctx", "tp"),
        P("ctx", "tp"),
        P("tp", None),
        P("tp", None),
        P("tp"),
        P("ctx", "tp"),
    )
    out_specs = (P("ctx", "tp"), P("ctx", "tp"), P("ctx", "tp"), P("ctx", "tp"), P("tp", None))
    return jax.shard_map(shards, mesh=mesh, in_specs=in_specs, out_specs=out_specs, check_vma=False)
```

profile of v0, /device:TPU:32, one launch (start us, length us, event | category | flops | bytes accessed | tf_op | source)
XLA Modules:
  0.0 280.1 jit_solution(7708082309188066356)
XLA Ops:
  0.6 1.0 copy.140
  1.7 1.1 copy.141
  3.5 15.9 %all-to-all-start = ((bf16[128,32,16]{0,2,1:T(8,128)(2,1)}), bf16[128,32,16]{0,2,1:T(8,128)(2,1)}, u32[]{:S(2)}, u32[]{:S(2)}) async-start(bf16[128,32,16]{0,2,1:T(8,128)(2,1)} %bitcast.8), calls=%async_computation | async-start | bytes 262144 | tf_op jit(solution)/shard_map/all_to_all | solution.py:128
  19.6 0.8 constant_dynamic-slice_fusion.1
  20.7 1.3 fusion.56
  23.1 1.1 rev.18
  24.3 54.4 %gather_fusion = f32[16384,16]{1,0:T(8,128)} fusion(f32[128,16]{1,0:T(8,128)S(1)} %bitcast.55, s32[16384]{0:T(1024)S(1)} %bitcast_clamp_fusion), kind=kCustom, calls=%fused_computation | custom fusion | bytes 2162688 | tf_op jit(solution)/shard_map/while/body/eval_jaxpr/gather | solution.py:24
  78.7 6.8 %copy.139 = f32[128,128,16]{0,1,2:T(8,128)S(1)} copy(f32[128,128,16]{2,1,0:T(8,128)} %bitcast.56) | data formatting | bytes 2097152 | tf_op jit(solution)/shard_map/while/body/eval_jaxpr/gather | solution.py:24
  86.2 2.2 fusion.10
  88.4 0.8 copy.146
  89.3 1.0 slice_add_fusion.1
  94.3 0.9 fusion.30
  97.1 1.5 fusion.14
  98.6 2.0 fusion.4
  101.4 12.2 %all-to-all-start.1 = ((bf16[32,128,16]{1,2,0:T(8,128)(2,1)}), bf16[32,128,16]{1,2,0:T(8,128)(2,1)S(1)}, u32[]{:S(2)}, u32[]{:S(2)}) async-start(bf16[32,128,16]{1,2,0:T(8,128)(2,1)} %copy.149), calls=%async_computation.1 | async-start | bytes 262144 | tf_op jit(solution)/shard_map/all_to_all | solution.py:139
  113.6 0.8 copy.135
  115.4 6.9 %all-to-all-done.1 = bf16[32,128,16]{1,2,0:T(8,128)(2,1)S(1)} async-done(((bf16[32,128,16]{1,2,0:T(8,128)(2,1)}), bf16[32,128,16]{1,2,0:T(8,128)(2,1)S(1)}, u32[]{:S(2)}, u32[]{:S(2)}) %all-to-all-start.1) | async-done | bytes 131104 | tf_op jit(solution)/shard_map/all_to_all | solution.py:139
  122.3 1.9 fusion.24
  124.2 8.2 %all-to-all-start.2 = ((bf16[128,32,16]{0,2,1:T(8,128)(2,1)}), bf16[128,32,16]{0,2,1:T(8,128)(2,1)S(1)}, u32[]{:S(2)}, u32[]{:S(2)}) async-start(bf16[128,32,16]{0,2,1:T(8,128)(2,1)} %bitcast.63), calls=%async_computation.2 | async-start | bytes 262144 | tf_op jit(solution)/shard_map/all_to_all | solution.py:142
  132.5 1.1 copy.184
  134.1 1.7 copy.178
  135.9 1.7 copy.165
  137.6 3.6 %all-to-all-done.2 = bf16[128,32,16]{0,2,1:T(8,128)(2,1)S(1)} async-done(((bf16[128,32,16]{0,2,1:T(8,128)(2,1)}), bf16[128,32,16]{0,2,1:T(8,128)(2,1)S(1)}, u32[]{:S(2)}, u32[]{:S(2)}) %all-to-all-start.2) | async-done | bytes 131104 | tf_op jit(solution)/shard_map/all_to_all | solution.py:142
  141.1 1.0 fusion.36
  142.1 1.7 copy.155
  143.8 1.0 fusion.57
  147.5 1.9 pad.116
  149.4 1.9 pad.117
  151.3 1.4 add.275
  152.7 1.4 fusion.41
  154.1 1.3 slice.495
  155.4 1.4 pad.119
  156.8 1.4 pad_maximum_fusion.5
  158.1 3.2 %pad.118 = f32[8,16,16]{2,1,0:T(8,128)} pad(f32[4,16,16]{2,1,0:T(8,128)} %pad_maximum_fusion.5, f32[]{:T(128)} %constant.76.clone.1), padding=0_1_1x0_0_0x0_0_0 | pad | bytes 12292 | tf_op jit(solution)/shard_map/while/body/eval_jaxpr/pad | solution.py:43
  161.3 0.9 fusion.39
  162.3 1.5 add.277
  163.8 1.6 slice.469
  166.0 1.3 fusion
  167.3 1.8 fusion.6
  169.2 1.1 fusion.5
  170.3 51.1 %all_gather.3 = f32[512,16]{1,0:T(8,128)S(1)} all-gather(f32[16,16]{1,0:T(8,128)S(1)} %add_multiply_fusion.6), channel_id=1, replica_groups=mesh['ctx'=32,'tp'=16] {'ctx'}, dimensions={0}, use_global_device_ids=true | all-gather | bytes 33792 | tf_op jit(solution)/shard_map/all_gather | solution.py:161
  222.7 0.9 fusion.12
  223.6 2.0 fusion.3
  226.3 7.4 %all-to-all-start.3 = ((bf16[32,128,16]{1,2,0:T(8,128)(2,1)}), bf16[32,128,16]{1,2,0:T(8,128)(2,1)S(1)}, u32[]{:S(2)}, u32[]{:S(2)}) async-start(bf16[32,128,16]{1,2,0:T(8,128)(2,1)} %copy.158), calls=%async_computation.3 | async-start | bytes 262144 | tf_op jit(solution)/shard_map/all_to_all | solution.py:151
  234.4 0.8 copy.166
  235.2 41.7 %psum.7 = f32[]{:T(128)} all-reduce(f32[]{:T(128)} %multiply_reduce_fusion), channel_id=1, replica_groups=mesh['ctx'=32,'tp'=16] {'tp'}, use_global_device_ids=true, to_apply=%region_1.2 | all-reduce | flops 1 | bytes 8 | tf_op jit(solution)/shard_map/psum | solution.py:162
  278.5 0.8 copy.167
  279.3 0.8 copy.168
  (130 shorter events, 17.9 us)
Async XLA Ops:
  0.6 18.8 %copy-start = (f32[512,16]{0,1:T(8,128)S(1)}, f32[512,16]{0,1:T(8,128)}, u32[]{:S(2)}) copy-start(f32[512,16]{0,1:T(8,128)} %param.10) | copy-start | bytes 98308
  1.7 19.0 %copy-start.2 = (bf16[128,512]{0,1:T(8,128)(2,1)}, bf16[128,512]{0,1:T(8,128)(2,1)S(1)}, u32[]{:S(2)}) copy-start(bf16[128,512]{0,1:T(8,128)(2,1)S(1)} %copy.140) | copy-start | bytes 393220
  2.8 17.9 %copy-start.4 = (bf16[128,512]{0,1:T(8,128)(2,1)}, bf16[128,512]{0,1:T(8,128)(2,1)S(1)}, u32[]{:S(2)}) copy-start(bf16[128,512]{0,1:T(8,128)(2,1)S(1)} %copy.141) | copy-start | bytes 393220
  3.5 82.7 %all-to-all-start = ((bf16[128,32,16]{0,2,1:T(8,128)(2,1)}), bf16[128,32,16]{0,2,1:T(8,128)(2,1)}, u32[]{:S(2)}, u32[]{:S(2)}) async-start(bf16[128,32,16]{0,2,1:T(8,128)(2,1)} %bitcast.8), calls=%async_computation | async-start | bytes 262144 | tf_op jit(solution)/shard_map/all_to_all | solution.py:128
  19.6 0.9 copy-start.15
  94.1 2.0 copy-start.23
  96.3 2.3 copy-start.1
  98.6 15.0 %copy-start.17 = (bf16[128,512]{1,0:T(8,128)(2,1)S(1)}, bf16[128,512]{1,0:T(8,128)(2,1)}, u32[]{:S(2)}) copy-start(bf16[128,512]{1,0:T(8,128)(2,1)} %param.7) | copy-start | bytes 393220
  98.6 15.8 %copy-start.18 = (bf16[128,512]{1,0:T(8,128)(2,1)S(1)}, bf16[128,512]{1,0:T(8,128)(2,1)}, u32[]{:S(2)}) copy-start(bf16[128,512]{1,0:T(8,128)(2,1)} %param.13) | copy-start | bytes 393220
  98.6 16.6 %copy-start.16 = (f32[16,16]{1,0:T(8,128)S(1)}, f32[16,16]{1,0:T(8,128)}, u32[]{:S(2)}) copy-start(f32[16,16]{1,0:T(8,128)} %copy-done.15) | copy-start | bytes 3076
  100.7 21.6 %copy-start.20 = (f32[512]{0:T(512)S(1)}, f32[512]{0:T(512)}, u32[]{:S(2)}) copy-start(f32[512]{0:T(512)} %param.12) | copy-start | bytes 6148
  101.4 20.9 %all-to-all-start.1 = ((bf16[32,128,16]{1,2,0:T(8,128)(2,1)}), bf16[32,128,16]{1,2,0:T(8,128)(2,1)S(1)}, u32[]{:S(2)}, u32[]{:S(2)}) async-start(bf16[32,128,16]{1,2,0:T(8,128)(2,1)} %copy.149), calls=%async_computation.1 | async-start | bytes 262144 | tf_op jit(solution)/shard_map/all_to_all | solution.py:139
  124.2 16.9 %all-to-all-start.2 = ((bf16[128,32,16]{0,2,1:T(8,128)(2,1)}), bf16[128,32,16]{0,2,1:T(8,128)(2,1)S(1)}, u32[]{:S(2)}, u32[]{:S(2)}) async-start(bf16[128,32,16]{0,2,1:T(8,128)(2,1)} %bitcast.63), calls=%async_computation.2 | async-start | bytes 262144 | tf_op jit(solution)/shard_map/all_to_all | solution.py:142
  144.9 0.7 copy-start.7
  144.9 0.7 copy-start.8
  145.6 0.6 copy-start.13
  161.3 6.0 %copy-start.9 = (f32[16,16,128]{2,1,0:T(8,128)S(1)}, f32[16,16,128]{2,1,0:T(8,128)}, u32[]{:S(2)}) copy-start(f32[16,16,128]{2,1,0:T(8,128)} %copy.184) | copy-start | bytes 393220
  166.0 3.1 %copy-start.10 = (f32[16,16,32]{2,1,0:T(8,128)S(1)}, f32[16,16,32]{2,1,0:T(8,128)}, u32[]{:S(2)}) copy-start(f32[16,16,32]{2,1,0:T(8,128)} %copy.178) | copy-start | bytes 98308
  169.1 52.2 %copy-start.19 = (f32[1,16,16]{2,1,0:T(8,128)S(1)}, f32[1,16,16]{2,1,0:T(8,128)}, u32[]{:S(2)}) copy-start(f32[1,16,16]{2,1,0:T(8,128)} %slice.495) | copy-start | bytes 3076
  169.2 52.3 %copy-start.14 = (f32[8,16,16]{2,1,0:T(8,128)S(1)}, f32[8,16,16]{2,1,0:T(8,128)}, u32[]{:S(2)}) copy-start(f32[8,16,16]{2,1,0:T(8,128)} %add.277) | copy-start | bytes 24580
  170.3 51.4 %copy-start.12 = (f32[15,16,16]{2,1,0:T(8,128)S(1)}, f32[15,16,16]{2,1,0:T(8,128)}, u32[]{:S(2)}) copy-start(f32[15,16,16]{2,1,0:T(8,128)} %slice.469) | copy-start | bytes 46084
  221.8 0.6 copy-start.22
  223.6 10.8 %copy-start.11 = (bf16[128,512]{0,1:T(8,128)(2,1)S(1)}, bf16[128,512]{0,1:T(8,128)(2,1)}, u32[]{:S(2)}) copy-start(bf16[128,512]{0,1:T(8,128)(2,1)} %get-tuple-element.74) | copy-start | bytes 393220
  225.6 52.8 %copy-start.3 = (bf16[128,512]{0,1:T(8,128)(2,1)S(1)}, bf16[128,512]{0,1:T(8,128)(2,1)}, u32[]{:S(2)}) copy-start(bf16[128,512]{0,1:T(8,128)(2,1)} %copy-done.2) | copy-start | bytes 393220
  225.6 52.8 %copy-start.5 = (bf16[128,512]{0,1:T(8,128)(2,1)S(1)}, bf16[128,512]{0,1:T(8,128)(2,1)}, u32[]{:S(2)}) copy-start(bf16[128,512]{0,1:T(8,128)(2,1)} %copy-done.4) | copy-start | bytes 393220
  225.6 52.7 %copy-start.6 = (bf16[128,512]{0,1:T(8,128)(2,1)S(1)}, bf16[128,512]{0,1:T(8,128)(2,1)}, u32[]{:S(2)}) copy-start(bf16[128,512]{0,1:T(8,128)(2,1)} %get-tuple-element.76) | copy-start | bytes 393220
  225.6 52.7 %copy-start.21 = (f32[512]{0:T(512)S(1)}, f32[512]{0:T(512)}, u32[]{:S(2)}) copy-start(f32[512]{0:T(512)} %param.12) | copy-start | bytes 6148
  226.3 52.0 %all-to-all-start.3 = ((bf16[32,128,16]{1,2,0:T(8,128)(2,1)}), bf16[32,128,16]{1,2,0:T(8,128)(2,1)S(1)}, u32[]{:S(2)}, u32[]{:S(2)}) async-start(bf16[32,128,16]{1,2,0:T(8,128)(2,1)} %copy.158), calls=%async_computation.3 | async-start | bytes 262144 | tf_op jit(solution)/shard_map/all_to_all | solution.py:151
where the time goes:
time: 282 us; the launch traced here: 280 us
  local copies, waits for them, and re-layouts  96.8 us (34%)
  blocking collectives  92.8 us (33%)
  starting transfers between devices  43.7 us (15%)
  other arithmetic  20.1 us (7%)
  matrix products  14.2 us (5%)
  waiting for transfers between devices  10.5 us (4%)
    gather x2, local copies, waits for them, and re-layouts, prepare(): short_filter[jnp.maximum(lag_table, 0)]  61.2 us
    all_gather x1, blocking collectives, shards(): raw_all = lax.all_gather(own_raw, 'ctx', axis=0, tiled=True)  51.1 us
    psum x1, blocking collectives, shards(): grad_square = lax.psum(jnp.sum(raw_all * raw_all), 'tp')  41.7 us
    all_to_all x1, starting transfers between devices, shards(): lax.all_to_all(gated, 'ctx', split_axis=1, concat_axis=0, tiled=True)  15.9 us
    unnamed x64, local copies, waits for them, and re-layouts  14 us
    all_to_all x1, starting transfers between devices, shards(): lax.all_to_all(conv_line.astype(jnp.bfloat16), 'ctx', split_axis=0, conca...  12.2 us
    pad x8, local copies, waits for them, and re-layouts, backward_states(): lax.associative_scan(chain_link, (decays[::-1], start_states[::-1]), axis=0)  8.84 us
    all_to_all x1, starting transfers between devices, shards(): lax.all_to_all(pulled, 'ctx', split_axis=1, concat_axis=0, tiled=True)  8.18 us
  transfers between devices with their start and end apart: 4, of which 2 were waited for; matrix products, arithmetic and copies ran while one was open for 27% of the time, Pallas kernels for 0%

commit v1 on v0

--- a/solution.py
+++ b/solution.py
@@ -158,7 +158,9 @@
     grad_gated = adjoint.astype(jnp.float32) + skip_gain[None, :] * pulled.astype(jnp.float32)
     grad_keys = (grad_gated * values_f).astype(jnp.bfloat16)
     grad_values = (grad_gated * keys_f).astype(jnp.bfloat16)
-    raw_all = lax.all_gather(own_raw, "ctx", axis=0, tiled=True)
+    raw_all = jnp.concatenate(
+        lax.all_to_all(jnp.stack([own_raw] * lax.axis_size("ctx")), "ctx", 0, 0), axis=0
+    )
     grad_square = lax.psum(jnp.sum(raw_all * raw_all), "tp")
     factor = jnp.minimum(1.0, math.sqrt(D * ORDER) / jnp.sqrt(grad_square + 1e-06))
     grad_residues = raw_all * factor

time: 282 us -> 299 us (1.060)
  blocking collectives: 92.8 us -> 41.7 us
  local copies, waits for them, and re-layouts: 96.8 us -> 136 us
  other arithmetic: 20.1 us -> 36 us
  starting transfers between devices: 43.7 us -> 57.4 us
    all_gather x1 -> x0, blocking collectives: 51.1 us -> none  [shards(): raw_all = lax.all_gather(own_raw, 'ctx', axis=0, tiled=True)]
    pad x8, local copies, waits for them, and re-layouts: 8.84 us -> 36.5 us  [backward_states(): lax.associative_scan(chain_link, (decays[::-1], start_states[::-1]), axis=0)]
    all_to_all x0 -> x1, starting transfers between devices: none -> 12.1 us  [shards(): lax.all_to_all(jnp.stack([own_raw] * lax.axis_size('ctx')), 'ctx', 0, 0)]
    all_to_all x0 -> x1, waiting for transfers between devices: none -> 3.55 us  [shards(): lax.all_to_all(jnp.stack([own_raw] * lax.axis_size('ctx')), 'ctx', 0, 0)]
    all_to_all x1, waiting for transfers between devices: 3.57 us -> 0.09 us  [shards(): lax.all_to_all(pulled, 'ctx', split_axis=1, concat_axis=0, tiled=True)]
    add x5, other arithmetic: 3.52 us -> 6.92 us  [backward_states(): lax.associative_scan(chain_link, (decays[::-1], start_states[::-1]), axis=0)]
    unnamed x64 -> x73, local copies, waits for them, and re-layouts: 14 us -> 16.7 us
  transfers between devices with their start and end apart: 4 -> 5, of which waited for: 2 -> 3; matrix products, arithmetic and copies ran while one was open for 27% -> 30% of each run, Pallas kernels for 0% -> 0%
where the time goes in v1:
time: 299 us; the launch traced here: 295 us
  local copies, waits for them, and re-layouts  136 us (45%)
  starting transfers between devices  57.4 us (19%)
  blocking collectives  41.7 us (14%)
  other arithmetic  36 us (12%)
  matrix products  13.6 us (5%)
  waiting for transfers between devices  8.78 us (3%)
    gather x2, local copies, waits for them, and re-layouts, prepare(): short_filter[jnp.maximum(lag_table, 0)]  61.2 us
    psum x1, blocking collectives, shards(): grad_square = lax.psum(jnp.sum(raw_all * raw_all), 'tp')  41.7 us
    pad x8, local copies, waits for them, and re-layouts, backward_states(): lax.associative_scan(chain_link, (decays[::-1], start_states[::-1]), axis=0)  36.5 us
    unnamed x73, local copies, waits for them, and re-layouts  16.7 us
    all_to_all x1, starting transfers between devices, shards(): lax.all_to_all(gated, 'ctx', split_axis=1, concat_axis=0, tiled=True)  15.8 us
    all_to_all x1, starting transfers between devices, shards(): lax.all_to_all(conv_line.astype(jnp.bfloat16), 'ctx', split_axis=0, conca...  12.2 us
    all_to_all x1, starting transfers between devices, shards(): lax.all_to_all(jnp.stack([own_raw] * lax.axis_size('ctx')), 'ctx', 0, 0)  12.1 us
    all_to_all x1, starting transfers between devices, shards(): lax.all_to_all(from_groups(adj_line).astype(jnp.bfloat16), 'ctx', split_a...  8.99 us
  transfers between devices with their start and end apart: 5, of which 3 were waited for; matrix products, arithmetic and copies ran while one was open for 30% of the time, Pallas kernels for 0%

profile of v1, /device:TPU:32, one launch (start us, length us, event | category | flops | bytes accessed | tf_op | source)
XLA Modules:
  0.0 295.5 jit_solution(12012188855948047977)
XLA Ops:
  3.5 15.8 %all-to-all-start = ((bf16[128,32,16]{0,2,1:T(8,128)(2,1)}), bf16[128,32,16]{0,2,1:T(8,128)(2,1)S(1)}, u32[]{:S(2)}, u32[]{:S(2)}) async-start(bf16[128,32,16]{0,2,1:T(8,128)(2,1)} %bitcast.6), calls=%async_computation | async-start | bytes 262144 | tf_op jit(solution)/shard_map/all_to_all | solution.py:128
  21.6 1.6 fusion.56
  23.8 54.4 %gather_fusion = f32[16384,16]{1,0:T(8,128)} fusion(f32[128,16]{1,0:T(8,128)S(1)} %bitcast.56, s32[16384]{0:T(1024)S(1)} %bitcast_clamp_fusion), kind=kCustom, calls=%fused_computation | custom fusion | bytes 2162688 | tf_op jit(solution)/shard_map/while/body/eval_jaxpr/gather | solution.py:24
  78.2 6.8 %copy.144 = f32[128,128,16]{0,1,2:T(8,128)S(1)} copy(f32[128,128,16]{2,1,0:T(8,128)} %bitcast.57) | data formatting | bytes 2097152 | tf_op jit(solution)/shard_map/while/body/eval_jaxpr/gather | solution.py:24
  85.1 2.3 rev.18
  88.0 2.3 fusion.10
  99.5 2.0 fusion.4
  102.2 12.2 %all-to-all-start.1 = ((bf16[32,128,16]{1,2,0:T(8,128)(2,1)}), bf16[32,128,16]{1,2,0:T(8,128)(2,1)S(1)}, u32[]{:S(2)}, u32[]{:S(2)}) async-start(bf16[32,128,16]{1,2,0:T(8,128)(2,1)} %copy.156), calls=%async_computation.1 | async-start | bytes 262144 | tf_op jit(solution)/shard_map/all_to_all | solution.py:139
  116.0 2.0 exponential_bitcast_fusion
  118.0 5.1 %all-to-all-done.1 = bf16[32,128,16]{1,2,0:T(8,128)(2,1)S(1)} async-done(((bf16[32,128,16]{1,2,0:T(8,128)(2,1)}), bf16[32,128,16]{1,2,0:T(8,128)(2,1)S(1)}, u32[]{:S(2)}, u32[]{:S(2)}) %all-to-all-start.1) | async-done | bytes 131104 | tf_op jit(solution)/shard_map/all_to_all | solution.py:139
  123.1 1.9 fusion.24
  125.0 8.2 %all-to-all-start.2 = ((bf16[128,32,16]{0,2,1:T(8,128)(2,1)}), bf16[128,32,16]{0,2,1:T(8,128)(2,1)S(1)}, u32[]{:S(2)}, u32[]{:S(2)}) async-start(bf16[128,32,16]{0,2,1:T(8,128)(2,1)} %bitcast.12), calls=%async_computation.2 | async-start | bytes 262144 | tf_op jit(solution)/shard_map/all_to_all | solution.py:142
  134.1 1.2 slice.512
  135.4 2.3 copy.196
  138.4 1.7 copy.189
  140.1 1.7 copy.175
  142.9 1.7 copy.162
  149.5 1.9 pad.117
  151.4 1.3 pad_maximum_fusion.7
  152.8 1.9 pad.116
  155.5 1.4 add.275
  156.9 1.3 pad_maximum_fusion.5
  158.2 3.2 %pad.118 = f32[8,16,16]{2,1,0:T(8,128)} pad(f32[4,16,16]{2,1,0:T(8,128)} %pad_maximum_fusion.5, f32[]{:T(128)} %constant.76.clone.1), padding=0_1_1x0_0_0x0_0_0 | pad | bytes 12292 | tf_op jit(solution)/shard_map/while/body/eval_jaxpr/pad | solution.py:43
  161.4 3.2 %pad.119 = f32[8,16,16]{2,1,0:T(8,128)} pad(f32[4,16,16]{2,1,0:T(8,128)} %add.275, f32[]{:T(128)} %constant.76.clone.1), padding=1_0_1x0_0_0x0_0_0 | pad | bytes 12292 | tf_op jit(solution)/shard_map/while/body/eval_jaxpr/pad | solution.py:43
  164.6 1.5 add.277
  166.2 1.5 fusion.39
  167.7 1.3 slice.495
  169.0 1.6 slice.469
  170.5 1.3 slice.494
  171.8 4.7 %pad.121 = f32[16,16,16]{2,1,0:T(8,128)} pad(f32[8,16,16]{2,1,0:T(8,128)} %add.277, f32[]{:T(128)} %constant.76.clone.1), padding=1_0_1x0_0_0x0_0_0 | pad | bytes 24580 | tf_op jit(solution)/shard_map/while/body/eval_jaxpr/pad | solution.py:43
  176.5 1.5 pad_maximum_fusion.3
  178.0 4.7 %pad.120 = f32[16,16,16]{2,1,0:T(8,128)} pad(f32[8,16,16]{2,1,0:T(8,128)} %pad_maximum_fusion.3, f32[]{:T(128)} %constant.76.clone.1), padding=0_1_1x0_0_0x0_0_0 | pad | bytes 24580 | tf_op jit(solution)/shard_map/while/body/eval_jaxpr/pad | solution.py:43
  182.6 1.6 add.279
  186.7 8.4 %pad.122 = f32[32,16,16]{2,1,0:T(8,128)} pad(f32[16,16,16]{2,1,0:T(8,128)} %pad_maximum_fusion.1, f32[]{:T(128)} %constant.76.clone.1), padding=0_1_1x0_0_0x0_0_0 | pad | bytes 49156 | tf_op jit(solution)/shard_map/while/body/eval_jaxpr/pad | solution.py:43
  195.2 8.4 %pad.123 = f32[32,16,16]{2,1,0:T(8,128)} pad(f32[16,16,16]{2,1,0:T(8,128)} %add.279, f32[]{:T(128)} %constant.76.clone.1), padding=1_0_1x0_0_0x0_0_0 | pad | bytes 49156 | tf_op jit(solution)/shard_map/while/body/eval_jaxpr/pad | solution.py:43
  203.6 1.8 add.281
  205.4 1.7 rev.20
  207.0 1.8 slice_add_fusion
  208.8 1.8 copy.201
  210.6 2.6 fusion.5
  213.2 1.4 copy.190
  215.4 1.8 fusion.6
  218.2 12.1 %all-to-all-start.4 = ((f32[32,1,256]{2,1,0:T(1,128)}), f32[32,1,256]{2,1,0:T(1,128)S(1)}, u32[]{:S(2)}, u32[]{:S(2)}) async-start(f32[32,1,256]{2,1,0:T(1,128)} %reshape.133), calls=%async_computation.4 | async-start | bytes 65536 | tf_op jit(solution)/shard_map/all_to_all | solution.py:162
  231.2 2.0 fusion.3
  233.9 3.5 %all-to-all-done.4 = f32[32,1,256]{2,1,0:T(1,128)S(1)} async-done(((f32[32,1,256]{2,1,0:T(1,128)}), f32[32,1,256]{2,1,0:T(1,128)S(1)}, u32[]{:S(2)}, u32[]{:S(2)}) %all-to-all-start.4) | async-done | bytes 32800 | tf_op jit(solution)/shard_map/all_to_all | solution.py:162
  237.5 9.0 %all-to-all-start.3 = ((bf16[32,128,16]{1,2,0:T(8,128)(2,1)}), bf16[32,128,16]{1,2,0:T(8,128)(2,1)S(1)}, u32[]{:S(2)}, u32[]{:S(2)}) async-start(bf16[32,128,16]{1,2,0:T(8,128)(2,1)} %copy.165), calls=%async_computation.3 | async-start | bytes 262144 | tf_op jit(solution)/shard_map/all_to_all | solution.py:151
  249.3 41.7 %psum.7 = f32[]{:T(128)} all-reduce(f32[]{:T(128)} %multiply_reduce_fusion.1), channel_id=1, replica_groups=mesh['ctx'=32,'tp'=16] {'tp'}, use_global_device_ids=true, to_apply=%region_1.2 | all-reduce | flops 1 | bytes 8 | tf_op jit(solution)/shard_map/psum | solution.py:164
  292.8 1.1 fusion.21
  (147 shorter events, 37.2 us)
Async XLA Ops:
  1.7 19.4 %copy-start.3 = (bf16[128,512]{0,1:T(8,128)(2,1)}, bf16[128,512]{0,1:T(8,128)(2,1)S(1)}, u32[]{:S(2)}) copy-start(bf16[128,512]{0,1:T(8,128)(2,1)S(1)} %copy.146) | copy-start | bytes 393220
  2.7 18.8 %copy-start.5 = (bf16[128,512]{0,1:T(8,128)(2,1)}, bf16[128,512]{0,1:T(8,128)(2,1)S(1)}, u32[]{:S(2)}) copy-start(bf16[128,512]{0,1:T(8,128)(2,1)S(1)} %copy.145) | copy-start | bytes 393220
  3.5 84.5 %all-to-all-start = ((bf16[128,32,16]{0,2,1:T(8,128)(2,1)}), bf16[128,32,16]{0,2,1:T(8,128)(2,1)S(1)}, u32[]{:S(2)}, u32[]{:S(2)}) async-start(bf16[128,32,16]{0,2,1:T(8,128)(2,1)} %bitcast.6), calls=%async_computation | async-start | bytes 262144 | tf_op jit(solution)/shard_map/all_to_all | solution.py:128
  20.2 1.4 copy-start.17
  21.0 0.6 copy-start.16
  21.1 76.6 %copy-start.15 = (f32[16,16]{1,0:T(8,128)}, f32[16,16]{1,0:T(8,128)S(1)}, u32[]{:S(2)}) copy-start(f32[16,16]{1,0:T(8,128)S(1)} %copy.142) | copy-start | bytes 3076
  23.2 74.1 %copy-start.14 = (f32[16,16]{1,0:T(8,128)}, f32[16,16]{1,0:T(8,128)S(1)}, u32[]{:S(2)}) copy-start(f32[16,16]{1,0:T(8,128)S(1)} %slice_bitcast_fusion) | copy-start | bytes 3076
  88.0 4.1 %copy-start.23 = (f32[16,16]{1,0:T(8,128)}, f32[16,16]{1,0:T(8,128)S(1)}, u32[]{:S(2)}) copy-start(f32[16,16]{1,0:T(8,128)S(1)} %get-tuple-element.73) | copy-start | bytes 3076
  88.0 4.1 %copy-start.22 = (f32[16,16]{1,0:T(8,128)}, f32[16,16]{1,0:T(8,128)S(1)}, u32[]{:S(2)}) copy-start(f32[16,16]{1,0:T(8,128)S(1)} %get-tuple-element.72) | copy-start | bytes 3076
  94.0 3.1 %copy-start.2 = (f32[16,16,32]{1,0,2:T(8,128)S(1)}, f32[16,16,32]{1,0,2:T(8,128)}, u32[]{:S(2)}) copy-start(f32[16,16,32]{1,0,2:T(8,128)} %copy.152) | copy-start | bytes 98308
  97.2 0.7 copy-start.27
  98.0 1.4 copy-start.1
  99.4 15.0 %copy-start.18 = (f32[16,16]{0,1:T(8,128)S(1)}, f32[16,16]{0,1:T(8,128)}, u32[]{:S(2)}) copy-start(f32[16,16]{0,1:T(8,128)} %copy-done.17) | copy-start | bytes 3076
  99.4 15.7 %copy-start.20 = (bf16[128,512]{1,0:T(8,128)(2,1)S(1)}, bf16[128,512]{1,0:T(8,128)(2,1)}, u32[]{:S(2)}) copy-start(bf16[128,512]{1,0:T(8,128)(2,1)} %param.13) | copy-start | bytes 393220
  99.4 15.8 %copy-start.21 = (bf16[128,512]{1,0:T(8,128)(2,1)S(1)}, bf16[128,512]{1,0:T(8,128)(2,1)}, u32[]{:S(2)}) copy-start(bf16[128,512]{1,0:T(8,128)(2,1)} %param.7) | copy-start | bytes 393220
  102.2 20.9 %all-to-all-start.1 = ((bf16[32,128,16]{1,2,0:T(8,128)(2,1)}), bf16[32,128,16]{1,2,0:T(8,128)(2,1)S(1)}, u32[]{:S(2)}, u32[]{:S(2)}) async-start(bf16[32,128,16]{1,2,0:T(8,128)(2,1)} %copy.156), calls=%async_computation.1 | async-start | bytes 262144 | tf_op jit(solution)/shard_map/all_to_all | solution.py:139
  116.0 17.7 %copy-start = (f32[128,16,16]{2,1,0:T(8,128)S(1)}, f32[128,16,16]{2,1,0:T(8,128)}, u32[]{:S(2)}) copy-start(f32[128,16,16]{2,1,0:T(8,128)} %get-tuple-element.70) | copy-start | bytes 393220
  125.0 16.9 %all-to-all-start.2 = ((bf16[128,32,16]{0,2,1:T(8,128)(2,1)}), bf16[128,32,16]{0,2,1:T(8,128)(2,1)S(1)}, u32[]{:S(2)}, u32[]{:S(2)}) async-start(bf16[128,32,16]{0,2,1:T(8,128)(2,1)} %bitcast.12), calls=%async_computation.2 | async-start | bytes 262144 | tf_op jit(solution)/shard_map/all_to_all | solution.py:142
  146.3 0.7 copy-start.7
  146.4 0.7 copy-start.8
  147.1 0.6 copy-start.13
  147.1 1.9 copy-start.12
  182.6 3.4 %copy-start.24 = (f32[1,16,16]{2,1,0:T(8,128)S(1)}, f32[1,16,16]{2,1,0:T(8,128)}, u32[]{:S(2)}) copy-start(f32[1,16,16]{2,1,0:T(8,128)} %slice.494) | copy-start | bytes 3076
  214.5 0.9 copy-start.9
  215.4 1.9 copy-start.19
  215.4 1.9 copy-start.25
  217.3 13.9 %copy-start.10 = (f32[31,16,16]{0,2,1:T(8,128)S(1)}, f32[31,16,16]{0,2,1:T(8,128)}, u32[]{:S(2)}) copy-start(f32[31,16,16]{0,2,1:T(8,128)} %copy.201) | copy-start | bytes 95236
  218.2 19.3 %all-to-all-start.4 = ((f32[32,1,256]{2,1,0:T(1,128)}), f32[32,1,256]{2,1,0:T(1,128)S(1)}, u32[]{:S(2)}, u32[]{:S(2)}) async-start(f32[32,1,256]{2,1,0:T(1,128)} %reshape.133), calls=%async_computation.4 | async-start | bytes 65536 | tf_op jit(solution)/shard_map/all_to_all | solution.py:162
  231.2 17.3 %copy-start.11 = (bf16[128,512]{0,1:T(8,128)(2,1)S(1)}, bf16[128,512]{0,1:T(8,128)(2,1)}, u32[]{:S(2)}) copy-start(bf16[128,512]{0,1:T(8,128)(2,1)} %get-tuple-element.76) | copy-start | bytes 393220
  237.5 55.3 %all-to-all-start.3 = ((bf16[32,128,16]{1,2,0:T(8,128)(2,1)}), bf16[32,128,16]{1,2,0:T(8,128)(2,1)S(1)}, u32[]{:S(2)}, u32[]{:S(2)}) async-start(bf16[32,128,16]{1,2,0:T(8,128)(2,1)} %copy.165), calls=%async_computation.3 | async-start | bytes 262144 | tf_op jit(solution)/shard_map/all_to_all | solution.py:151
  247.7 45.1 %copy-start.4 = (bf16[128,512]{0,1:T(8,128)(2,1)S(1)}, bf16[128,512]{0,1:T(8,128)(2,1)}, u32[]{:S(2)}) copy-start(bf16[128,512]{0,1:T(8,128)(2,1)} %copy-done.3) | copy-start | bytes 393220
  247.7 45.1 %copy-start.6 = (bf16[128,512]{0,1:T(8,128)(2,1)S(1)}, bf16[128,512]{0,1:T(8,128)(2,1)}, u32[]{:S(2)}) copy-start(bf16[128,512]{0,1:T(8,128)(2,1)} %copy-done.5) | copy-start | bytes 393220
  247.8 45.1 %copy-start.26 = (f32[512]{0:T(512)S(1)}, f32[512]{0:T(512)}, u32[]{:S(2)}) copy-start(f32[512]{0:T(512)} %param.12) | copy-start | bytes 6148
